TPU v7x, 256 devices: a whole 4x4x8 slice. The times are simulated.
256 devices in a mesh: loop: 64 (over y, z_lo, x, core), occ: 4 (over z_hi).
Axes of the slice: x: 4, y: 4, z: 8 (z_hi: 4, z_lo: 2; z = z_hi * 2 + z_lo), core: 2. Of those that a mesh axis runs over, the one named last changes fastest.
Arguments:
- integrals: bfloat16 [131072, 8192], P('loop', 'occ'), may hold values from -0.0625 to 0.0625
- amplitudes: bfloat16 [512, 8192], P('loop', 'occ'), may hold values from -6 to 6
- tile_list: int32 [512, 2], P('loop'), may hold values from -1 to 49, as said below
- occ_pairs: int32 [512, 2], replicated, may hold values from 0 to 199
- e_occ: float32 [200], replicated, may hold values from -1.5 to -0.3
- e_virt: float32 [800], replicated, may hold values from 0.2 to 2
Outputs:
- increment: float32 [512, 131072], P('occ', 'loop')
Inputs may be any that keep to these rules, and one draw needn't show every extreme that they name: tile_list[q] and tile_list[q + 256] are (A, B) and (B, A) with A != B, or both (-1, -1). Live tiles are distinct and lie in one pair-symmetry sector of the orbital tiles' irreps; the first 8 slots are live; at most three quarters of the slots are live.
All inputs are finite; a program needn't handle non-finite values.
Results may differ from a plain program's by a relative error of at most 0.014.
Values may be sent and summed in bfloat16 or wider, within the bound.
A program may use at most 64 MiB of HBM per device.

v0:
```python
import jax
import jax.numpy as jnp
from jax import lax
from jax.sharding import PartitionSpec as P

TILE = 16


def shifted(array, axis, by):
    devices = lax.axis_size(axis)
    return lax.ppermute(array, axis, [(i, (i + by) % devices) for i in range(devices)])


def flip_tiles(values, tiles):
    count = values.shape[0]
    shaped = values.reshape(count, tiles, TILE, TILE)
    return jnp.swapaxes(shaped, 2, 3).reshape(count, tiles * TILE * TILE)


def lookup(indices, table):
    matches = indices[..., None] == jnp.arange(table.shape[0], dtype=jnp.int32)
    return jnp.sum(jnp.where(matches, table, 0.0), axis=-1)


def per_device(integrals, amplitudes, tile_list, occ_pairs, e_occ, e_virt):
    tiles = tile_list.shape[0]
    width = TILE * TILE
    live = tile_list[:, 0] >= 0
    result = lax.dot_general(
        lax.all_gather(amplitudes, "loop", axis=0, tiled=True),
        integrals,
        (((1,), (1,)), ((), ())),
        preferred_element_type=jnp.float32,
    )
    partials = result.astype(jnp.bfloat16)
    half = lax.axis_size("loop") // 2
    mirrored = shifted(partials, "loop", half)
    combined = partials.astype(jnp.float32) + flip_tiles(mirrored, tiles).astype(jnp.float32)
    summed = lax.psum_scatter(
        combined.astype(jnp.bfloat16), "occ", scatter_dimension=0, tiled=True
    ).astype(jnp.float32)
    share = summed.shape[0]
    my_pairs = lax.dynamic_slice_in_dim(occ_pairs, lax.axis_index("occ") * share, share, 0)
    pair_energy = lookup(my_pairs[:, 0], e_occ) + lookup(my_pairs[:, 1], e_occ)
    offsets = jnp.arange(TILE, dtype=jnp.int32)[None, :]
    first = lookup(tile_list[:, 0:1] * TILE + offsets, e_virt)
    second = lookup(tile_list[:, 1:2] * TILE + offsets, e_virt)
    row_energy = (first[:, :, None] + second[:, None, :]).reshape(-1)
    denom = pair_energy[:, None] - row_energy[None, :]
    live_rows = jnp.repeat(live, width)
    return jnp.where(live_rows[None, :], summed / denom, 0.0)


def solution(mesh):
    placed = (P("loop", "occ"), P("loop", "occ"), P("loop", None), P(), P(), P())
    return jax.shard_map(
        per_device, mesh=mesh, in_specs=placed, out_specs=P("occ", "loop"), check_vma=False
    )
```

profile of v0, /device:TPU:4, one launch (start us, length us, event | category | flops | bytes accessed | tf_op | source)
XLA Modules:
  0.0 255.0 jit_solution(8605739127782768165)
XLA Ops:
  6.5 0.0 copy-start
  6.5 0.0 all-gather.2.cloned.1.call-start
  6.5 0.7 all-gather.2.cloned.1.call-update
  7.3 0.0 reduce-scatter.2.cloned.1.call-start
  7.3 109.7 %all-gather.2.cloned.1.call-done = bf16[512,2048]{1,0:T(8,128)(2,1)} async-done(((bf16[8,2048]{1,0:T(8,128)(2,1)}), bf16[512,2048]{1,0:T(8,128)(2,1)}) %all-gather.2.cloned.1.call-update) | async-done | bytes 2097168 | tf_op jit(solution)/shard_map/all_gather | solution.py:30
  117.0 8.5 %convolution_convert_fusion = bf16[512,2048]{1,0:T(8,128)(2,1)S(1)} fusion(bf16[512,2048]{1,0:T(8,128)(2,1)} %all-gather.2.cloned.1.call-done, bf16[2048,2048]{1,0:T(8,128)(2,1)} %param.6), kind=kOutput, calls=%fused_computation.1 | convolution fusion | flops 4296015872 | bytes 12582912 | tf_op jit(solution)/shard_map/dot_general | solution.py:29
  125.6 0.0 copy-start.1
  125.6 1.3 copy-done.1
  126.9 2.1 collective-permute-start
  129.0 47.2 %collective-permute-done = bf16[512,2048]{1,0:T(8,128)(2,1)S(1)} collective-permute-done((bf16[512,2048]{1,0:T(8,128)(2,1)S(1)}, bf16[512,2048]{1,0:T(8,128)(2,1)S(1)}, u32[]{:S(2)}, u32[]{:S(2)}) %collective-permute-start) | collective-permute-done | bytes 2097184 | tf_op jit(solution)/shard_map/ppermute | solution.py:11
  176.2 3.0 %copy.11 = f32[512,2048]{0,1:T(8,128)} copy(bf16[512,2048]{1,0:T(8,128)(2,1)S(1)} %collective-permute-done) | data formatting | bytes 6291456 | tf_op jit(solution)/shard_map/convert_element_type | solution.py:38
  179.2 6.6 %copy.12 = f32[512,8,16,16]{0,3,2,1:T(8,128)} copy(f32[512,8,16,16]{0,2,3,1:T(8,128)} %bitcast.16) | data formatting | bytes 8388608 | tf_op jit(solution)/shard_map/convert_element_type | solution.py:38
  185.8 0.0 copy-start.2
  185.8 5.5 %copy.13 = f32[512,2048]{1,0:T(8,128)} copy(f32[512,2048]{0,1:T(8,128)} %bitcast.17) | data formatting | bytes 8388608 | tf_op jit(solution)/shard_map/convert_element_type | solution.py:38
  191.3 0.0 copy-done.2
  191.3 0.0 copy-start.5
  191.3 0.0 copy-start.3
  191.3 0.0 copy-start.4
  191.3 4.3 %add_convert_fusion = bf16[512,2048]{1,0:T(8,128)(2,1)} fusion(f32[512,2048]{1,0:T(8,128)} %copy.13, bf16[512,2048]{1,0:T(8,128)(2,1)S(1)} %copy-done.2), kind=kLoop, calls=%fused_computation | loop fusion | flops 3145728 | bytes 8388608 | tf_op jit(solution)/shard_map/convert_element_type | solution.py:40
  195.6 0.0 reduce-scatter.2.cloned.1.call-update
  195.6 0.0 copy-done.5
  195.6 0.1 iota_add_fusion
  195.7 0.0 copy-done.3
  195.7 0.2 select_reduce_fusion.1
  195.9 0.1 broadcast_add_fusion
  196.0 0.1 add.81
  196.1 0.1 broadcast_in_dim.47
  196.2 0.0 copy-done
  196.2 0.0 copy-done.4
  196.3 0.1 select_reduce_fusion.2
  196.4 49.5 %reduce-scatter.2.cloned.1.call-done = bf16[128,2048]{1,0:T(8,128)(2,1)} async-done(((bf16[512,2048]{1,0:T(8,128)(2,1)}), bf16[128,2048]{1,0:T(8,128)(2,1)}) %reduce-scatter.2.cloned.1.call-update) | async-done | bytes 524304 | tf_op jit(solution)/shard_map/reduce_scatter | solution.py:39
  245.9 2.3 divide_select_fusion
  (6 shorter events, 0.0 us)
Async XLA Ops:
  6.5 189.7 %copy-start = (s32[512,2]{0,1:T(2,128)S(1)}, s32[512,2]{0,1:T(2,128)}, u32[]{:S(2)}) copy-start(s32[512,2]{0,1:T(2,128)} %param.9) | copy-start | bytes 12292
  6.5 110.5 %all-gather.2.cloned.1.call-start = ((), (), s32[]{:S(2)}) async-start(), calls=%async_computation.1 | async-start | bytes 2129920 | tf_op jit(solution)/shard_map/all_gather | solution.py:30
  7.3 238.6 %reduce-scatter.2.cloned.1.call-start = ((), (), s32[]{:S(2)}) async-start(), calls=%async_computation.2 | async-start | bytes 2621440 | tf_op jit(solution)/shard_map/reduce_scatter | solution.py:39
  125.6 1.4 copy-start.1
  126.9 49.3 %collective-permute-start = (bf16[512,2048]{1,0:T(8,128)(2,1)S(1)}, bf16[512,2048]{1,0:T(8,128)(2,1)S(1)}, u32[]{:S(2)}, u32[]{:S(2)}) collective-permute-start(bf16[512,2048]{1,0:T(8,128)(2,1)S(1)} %convolution_convert_fusion), channel_id=1, source_target_pairs={{0,128},{4,132},{8,136},{12,140},{16,144},{20,148},{24,152},{28,15... | collective-permute-start | bytes 6291464 | tf_op jit(solution)/shard_map/ppermute | solution.py:11
  185.8 5.5 %copy-start.2 = (bf16[512,2048]{1,0:T(8,128)(2,1)S(1)}, bf16[512,2048]{1,0:T(8,128)(2,1)}, u32[]{:S(2)}) copy-start(bf16[512,2048]{1,0:T(8,128)(2,1)} %copy-done.1) | copy-start | bytes 6291460
  191.3 4.3 %copy-start.5 = (s32[8,2]{0,1:T(2,128)S(1)}, s32[8,2]{0,1:T(2,128)}, u32[]{:S(2)}) copy-start(s32[8,2]{0,1:T(2,128)} %param.8) | copy-start | bytes 196
  191.3 4.4 %copy-start.3 = (f32[800]{0:T(1024)S(1)}, f32[800]{0:T(1024)}, u32[]{:S(2)}) copy-start(f32[800]{0:T(1024)} %param.11) | copy-start | bytes 9604
  191.3 4.9 %copy-start.4 = (f32[200]{0:T(256)S(1)}, f32[200]{0:T(256)}, u32[]{:S(2)}) copy-start(f32[200]{0:T(256)} %param.10) | copy-start | bytes 2404
Sparse Core Ops, SparseCore 0:
  9.2 107.7 all-gather.1
  195.7 50.1 reduce-scatter.1
where the time goes:
time: 256 us; the launch traced here: 255 us
  waiting for transfers between devices  207 us (81%)
  local copies, waits for them, and re-layouts  16.7 us (7%)
  between operations  13.5 us (5%)
  matrix products  8.54 us (3%)
  other arithmetic  7.07 us (3%)
    all_gather x1, waiting for transfers between devices, per_device(): lax.all_gather(amplitudes, 'loop', axis=0, tiled=True)  110 us
    reduce_scatter x1, waiting for transfers between devices, per_device(): lax.psum_scatter(combined.astype(jnp.bfloat16), 'occ', scatter_dimension=...  49.5 us
    ppermute x1, waiting for transfers between devices, shifted(): lax.ppermute(array, axis, [(i, (i + by) % devices) for i in range(devices)])  47.2 us
    convert_element_type x3, local copies, waits for them, and re-layouts, per_device(): flip_tiles(mirrored, tiles).astype(jnp.float32)  15.1 us
    dot_general x1, matrix products, per_device(): lax.dot_general(lax.all_gather(amplitudes, 'loop', axis=0, tiled=True), i...  8.54 us
  transfers between devices with their start and end apart: 3, of which 3 were waited for; matrix products, arithmetic and copies ran while one was open for 0% of the time, Pallas kernels for 0%

commit v1 on v0

v1 whole, which is shorter than its diff:
```python
import functools

import jax
import jax.numpy as jnp
from jax import lax
from jax.experimental import pallas as pl
from jax.experimental.pallas import tpu as pltpu
from jax.sharding import PartitionSpec as P

MESH = pl.DeviceIdType.MESH
TILE = 16
WIDTH = TILE * TILE
ROWS = 2048
TILES = ROWS // WIDTH
CD = 2048
HALF = CD // 2
PAIRS = 512
SHARE = 128
NY, NZL, NX, NCORE, NOCC = 4, 2, 4, 2, 4
CHUNK = 128
GROUP = 16
STEP = 512
X_OFF = (0, 1, -1, 2)
BLOCKS = [(dy, dz) for dy in (0, 1, 3, 2) for dz in range(NZL)][1:]
BF16, F32 = jnp.bfloat16, jnp.float32


def kernel(
    ints_hbm, amps_ref, tiles_ref, pairs_ref, e_occ_ref, e_virt_ref, out_hbm,
    ints, own, peer, gath, part, sum1, sum2, low, mirr, outs, inv, pair_e, perm,
    load_sem, store_sem, sib_sem, blk_s, blk_r, fwd_s, fwd_r, x_s, x_r, xf_s, xf_r, z_s, z_r, m_s, m_r,
):
    loop, occ = lax.axis_index("loop"), lax.axis_index("occ")
    core, x, zl, y = loop % 2, (loop // 2) % NX, (loop // 8) % NZL, loop // 16

    def at(dy=0, dz=0, dx=0, dc=0, dh=0):
        yy, zz = (y + dy + NY) % NY, (zl + dz) % NZL
        xx, cc = (x + dx + NX) % NX, (core + dc) % NCORE
        return ((yy * NZL + zz) * NX + xx) * NCORE + cc, (occ + dh + NOCC) % NOCC

    sends = []

    def send(src, dst, send_sem, recv_sem, to):
        copy = pltpu.make_async_remote_copy(
            src_ref=src, dst_ref=dst, send_sem=send_sem, recv_sem=recv_sem,
            device_id=to, device_id_type=MESH,
        )
        copy.start()
        sends.append(copy)
        return copy

    load = pltpu.make_async_copy(ints_hbm, ints, load_sem)
    load.start()

    partners = [at(dc=1), at(dh=1), at(dh=-1)]
    partners += [at(dx=d) for d in X_OFF[1:]]
    partners += [at(dy=dy, dz=dz) for dy, dz in BLOCKS]
    barrier = pltpu.get_barrier_semaphore()
    for partner in partners:
        pl.semaphore_signal(barrier, inc=1, device_id=partner, device_id_type=MESH)
    block = amps_ref[...].astype(F32)
    doubled = jnp.concatenate([block, block], axis=0)
    own[...] = doubled.astype(BF16)
    pl.semaphore_wait(barrier, len(partners))

    swap = send(own, peer, sib_sem.at[0], sib_sem.at[1], at(dc=1))
    swap.wait_recv()
    upper = lax.broadcasted_iota(jnp.int32, (GROUP, CD), 0) < 8
    mine = jnp.logical_xor(upper, core == 1)
    merged = jnp.where(mine, doubled, peer[...].astype(F32)).astype(BF16)

    def block_rows(dy, dz):
        index = ((y + dy + NY) % NY) * NZL + (zl + dz) % NZL
        return pl.ds(pl.multiple_of(index * GROUP, GROUP), GROUP)

    here = block_rows(0, 0)
    gath[0, 0, here, :] = merged[:, :HALF]
    gath[0, 1, here, :] = merged[:, HALF:]

    blocks = []
    for i, (dy, dz) in enumerate(BLOCKS):
        mine_at = gath.at[0, core, here, :]
        blocks.append(send(mine_at, mine_at, blk_s.at[i], blk_r.at[i], at(dy=dy, dz=dz)))

    row_at = lax.broadcasted_iota(jnp.int32, (WIDTH, WIDTH), 0)
    col_at = lax.broadcasted_iota(jnp.int32, (WIDTH, WIDTH), 1)
    hit = col_at == (row_at % TILE) * TILE + row_at // TILE
    perm[...] = jnp.where(hit, 1.0, 0.0).astype(BF16)
    sub = lax.broadcasted_iota(jnp.int32, (8, 128), 0)

    def pair_body(g, carry):
        rows = jnp.zeros((8, 128), F32)
        for i in range(8):
            pair = occ * SHARE + g * 8 + i
            energy = e_occ_ref[pairs_ref[0, pair]] + e_occ_ref[pairs_ref[1, pair]]
            rows = jnp.where(sub == i, energy, rows)
        pair_e[pl.ds(pl.multiple_of(g * 8, 8), 8), :] = rows
        return carry

    lax.fori_loop(0, SHARE // 8, pair_body, 0)
    lane = lax.broadcasted_iota(jnp.int32, (8, WIDTH), 1)
    lane_x, lane_y = lane // TILE, lane % TILE

    def tile_body(t, carry):
        first, second = tiles_ref[0, t], tiles_ref[1, t]
        a, b = jnp.maximum(first, 0) * TILE, jnp.maximum(second, 0) * TILE
        e_a = jnp.zeros((8, WIDTH), F32)
        e_b = jnp.zeros((8, WIDTH), F32)
        for i in range(TILE):
            e_a = jnp.where(lane_x == i, e_virt_ref[a + i], e_a)
            e_b = jnp.where(lane_y == i, e_virt_ref[b + i], e_b)
        energy = e_a + e_b
        keep = jnp.full((8, WIDTH), first, jnp.int32) >= 0
        for g in range(SHARE // 8):
            pair = pair_e[g * 8:(g + 1) * 8, :]
            denom = jnp.concatenate([pair, pair], axis=1) - energy
            columns = pl.ds(pl.multiple_of(t * WIDTH, WIDTH), WIDTH)
            inv[g * 8:(g + 1) * 8, columns] = jnp.where(keep, 1.0 / denom, 0.0)
        return carry

    lax.fori_loop(0, TILES, tile_body, 0)

    forwards = []
    for i, (dy, dz) in enumerate(BLOCKS):
        blocks[i].wait_recv()
        there = gath.at[0, core, block_rows(-dy, -dz), :]
        forwards.append(send(there, there, fwd_s.at[i], fwd_r.at[i], at(dc=1)))
    spread = []
    for j in range(1, NX):
        spread.append(send(gath.at[0, core], gath.at[j, core], x_s.at[j - 1], x_r.at[j - 1], at(dx=-X_OFF[j])))
    for copy in forwards:
        copy.wait_recv()
    load.wait()

    def multiply(j):
        def body(n, carry):
            rows = pl.ds(pl.multiple_of(n * STEP, STEP), STEP)
            dims = (((1,), (1,)), ((), ()))
            product = lax.dot_general(gath[j, 0], ints[rows, :HALF], dims, preferred_element_type=F32)
            product += lax.dot_general(gath[j, 1], ints[rows, HALF:], dims, preferred_element_type=F32)
            rounded = product.astype(BF16)
            for k in range(NOCC):
                for g in range(2):
                    first = (k * 2 + g) * GROUP
                    part[j, k, g, :, rows] = rounded[first:first + GROUP]
            return carry

        lax.fori_loop(0, ROWS // STEP, body, 0)

    up, down, far = (occ + 1) % NOCC, (occ + 3) % NOCC, (occ + 2) % NOCC
    z = [[None] * 6 for _ in range(NX)]
    mirrors = [None] * NX

    def first_stage(j):
        plan = [
            (part.at[j, far, 0], sum1.at[j, 0], 1),
            (part.at[j, far, 1], sum1.at[j, 1], -1),
            (part.at[j, up, 1], sum2.at[j, 0, 1], 1),
            (part.at[j, down, 0], sum2.at[j, 1, 0], -1),
        ]
        for i, (src, dst, to) in enumerate(plan):
            z[j][i] = send(src, dst, z_s.at[j, i], z_r.at[j, i], at(dh=to))

    def second_stage(j):
        z[j][0].wait_recv()
        part[j, up, 0] = (part[j, up, 0].astype(F32) + sum1[j, 0].astype(F32)).astype(BF16)
        z[j][4] = send(part.at[j, up, 0], sum2.at[j, 0, 0], z_s.at[j, 4], z_r.at[j, 4], at(dh=1))
        z[j][1].wait_recv()
        part[j, down, 1] = (part[j, down, 1].astype(F32) + sum1[j, 1].astype(F32)).astype(BF16)
        z[j][5] = send(part.at[j, down, 1], sum2.at[j, 1, 1], z_s.at[j, 5], z_r.at[j, 5], at(dh=-1))

    def ladder(j):
        for i in range(2, 6):
            z[j][i].wait_recv()
        for g in range(2):
            total = part[j, occ, g].astype(F32) + sum2[j, 0, g].astype(F32) + sum2[j, 1, g].astype(F32)
            outs[j, g] = total
            low[j, g] = total.astype(BF16)
        mirrors[j] = send(low.at[j], mirr.at[j], m_s.at[j], m_r.at[j], at(dy=2))

    stores = []

    def finish(j):
        mirrors[j].wait_recv()
        xx = (x + X_OFF[j] + NX) % NX
        for g in range(2):
            stack = jnp.concatenate([mirr[j, g, :, t * WIDTH:(t + 1) * WIDTH] for t in range(TILES)], axis=0)
            flipped = jnp.dot(stack, perm[...], preferred_element_type=F32)
            rows = pl.ds(pl.multiple_of(g * 64 + xx * GROUP, GROUP), GROUP)
            for t in range(TILES):
                columns = slice(t * WIDTH, (t + 1) * WIDTH)
                total = outs[j, g, :, columns] + flipped[t * GROUP:(t + 1) * GROUP]
                outs[j, g, :, columns] = total * inv[rows, columns]
            store = pltpu.make_async_copy(outs.at[j, g], out_hbm.at[rows, :], store_sem.at[j, g])
            store.start()
            stores.append(store)

    def arrive(j):
        spread[j - 1].wait_recv()
        there = gath.at[j, core]
        send(there, there, xf_s.at[j - 1], xf_r.at[j - 1], at(dc=1)).wait_recv()

    multiply(0)
    first_stage(0)
    arrive(1)
    multiply(1)
    first_stage(1)
    second_stage(0)
    arrive(2)
    multiply(2)
    first_stage(2)
    ladder(0)
    second_stage(1)
    arrive(3)
    multiply(3)
    first_stage(3)
    ladder(1)
    second_stage(2)
    finish(0)
    ladder(2)
    second_stage(3)
    finish(1)
    ladder(3)
    finish(2)
    finish(3)
    for copy in sends:
        copy.wait_send()
    for store in stores:
        store.wait()


def per_device(integrals, amplitudes, tile_list, occ_pairs, e_occ, e_virt):
    dma = pltpu.SemaphoreType.DMA
    any_space = pl.BlockSpec(memory_space=pl.ANY)
    vmem = pl.BlockSpec(memory_space=pltpu.VMEM)
    smem = pl.BlockSpec(memory_space=pltpu.SMEM)
    return pl.pallas_call(
        kernel,
        out_shape=jax.ShapeDtypeStruct((SHARE, ROWS), F32),
        in_specs=[any_space, vmem, smem, smem, smem, smem],
        out_specs=any_space,
        scratch_shapes=[
            pltpu.VMEM((ROWS, CD), BF16),
            pltpu.VMEM((GROUP, CD), BF16),
            pltpu.VMEM((GROUP, CD), BF16),
            pltpu.VMEM((NX, 2, CHUNK, HALF), BF16),
            pltpu.VMEM((NX, NOCC, 2, GROUP, ROWS), BF16),
            pltpu.VMEM((NX, 2, GROUP, ROWS), BF16),
            pltpu.VMEM((NX, 2, 2, GROUP, ROWS), BF16),
            pltpu.VMEM((NX, 2, GROUP, ROWS), BF16),
            pltpu.VMEM((NX, 2, GROUP, ROWS), BF16),
            pltpu.VMEM((NX, 2, GROUP, ROWS), F32),
            pltpu.VMEM((SHARE, ROWS), F32),
            pltpu.VMEM((SHARE, 128), F32),
            pltpu.VMEM((WIDTH, WIDTH), BF16),
            dma,
            dma((NX, 2)),
            dma((2,)),
            dma((len(BLOCKS),)), dma((len(BLOCKS),)),
            dma((len(BLOCKS),)), dma((len(BLOCKS),)),
            dma((NX - 1,)), dma((NX - 1,)),
            dma((NX - 1,)), dma((NX - 1,)),
            dma((NX, 6)), dma((NX, 6)),
            dma((NX,)), dma((NX,)),
        ],
        compiler_params=pltpu.CompilerParams(
            collective_id=0, has_side_effects=True, vmem_limit_bytes=48 << 20
        ),
        cost_estimate=pl.CostEstimate(flops=2 * PAIRS * ROWS * CD, bytes_accessed=10 << 20, transcendentals=0),
    )(integrals, amplitudes, tile_list.T, occ_pairs.T, e_occ, e_virt)


def solution(mesh):
    placed = (P("loop", "occ"), P("loop", "occ"), P("loop", None), P(), P(), P())
    return jax.shard_map(
        per_device, mesh=mesh, in_specs=placed, out_specs=P("occ", "loop"), check_vma=False
    )
```

time: 256 us -> 74.7 us (0.29)
  waiting for transfers between devices: 207 us -> 0 us
  Pallas kernels: 0 us -> 69.2 us
  between operations: 13.5 us -> 0.01 us
  local copies, waits for them, and re-layouts: 16.7 us -> 4.46 us
  matrix products: 8.54 us -> 0 us
  other arithmetic: 7.07 us -> 0 us
    all_gather x1 -> x0, waiting for transfers between devices: 110 us -> none  [per_device(): lax.all_gather(amplitudes, 'loop', axis=0, tiled=True)]
    pallas_call x0 -> x1, Pallas kernels: none -> 69.2 us  [per_device(): pl.pallas_call(kernel, out_shape=jax.ShapeDtypeStruct((SHARE, ROWS), F32)...]
    reduce_scatter x1 -> x0, waiting for transfers between devices: 49.5 us -> none  [per_device(): lax.psum_scatter(combined.astype(jnp.bfloat16), 'occ', scatter_dimension=...]
    ppermute x1 -> x0, waiting for transfers between devices: 47.2 us -> none  [shifted(): lax.ppermute(array, axis, [(i, (i + by) % devices) for i in range(devices)])]
    convert_element_type x3 -> x0, local copies, waits for them, and re-layouts: 15.1 us -> none  [per_device(): flip_tiles(mirrored, tiles).astype(jnp.float32)]
    dot_general x1 -> x0, matrix products: 8.54 us -> none  [per_device(): lax.dot_general(lax.all_gather(amplitudes, 'loop', axis=0, tiled=True), i...]
    convert_element_type x1 -> x0, other arithmetic: 4.25 us -> none  [per_device(): combined.astype(jnp.bfloat16)]
    unnamed x12 -> x11, local copies, waits for them, and re-layouts: 1.37 us -> 4.46 us
  transfers between devices with their start and end apart: 3 -> 0, of which waited for: 3 -> 0; matrix products, arithmetic and copies ran while one was open for 0% -> 0% of each run, Pallas kernels for 0% -> 0%
where the time goes in v1:
time: 74.7 us; the launch traced here: 73.6 us
  Pallas kernels  69.2 us (93%)
  local copies, waits for them, and re-layouts  4.46 us (6%)
    pallas_call x1, Pallas kernels, per_device(): pl.pallas_call(kernel, out_shape=jax.ShapeDtypeStruct((SHARE, ROWS), F32)...  69.2 us
    unnamed x11, local copies, waits for them, and re-layouts  4.46 us

profile of v1, /device:TPU:4, one launch (start us, length us, event | category | flops | bytes accessed | tf_op | source)
XLA Modules:
  0.0 73.6 jit_solution(9522774054162120399)
XLA Ops:
  0.0 0.0 copy-start
  0.0 0.8 %copy-done = bf16[8,2048]{1,0:T(8,128)(2,1)S(1)} copy-done((bf16[8,2048]{1,0:T(8,128)(2,1)S(1)}, bf16[8,2048]{1,0:T(8,128)(2,1)}, u32[]{:S(2)}) %copy-start) | copy-done | bytes 32792
  0.8 0.0 copy-start.1
  0.8 0.7 copy-done.1
  1.4 0.0 copy-start.2
  1.4 0.7 copy-done.2
  2.1 0.0 copy-start.3
  2.1 0.7 copy-done.3
  2.8 0.0 copy-start.4
  2.8 0.7 copy-done.4
  3.5 69.2 %shard_map.64 = f32[128,2048]{1,0:T(8,128)S(1)} custom-call(bf16[2048,2048]{1,0:T(8,128)(2,1)} %ints_hbm.1, bf16[8,2048]{1,0:T(8,128)(2,1)S(1)} %copy-done, s32[2,8]{1,0:T(2,128)S(1)} %bitcast.3, s32[2,512]{1,0:T(2,128)S(1)} %bitcast.2, f32[200]{0:T(256)S(1)} %copy-done.4, f32[800]{0:T(1024)S(1)} %copy-done.2), custom_call_target="tpu_custom_call" | custom-call | flops 4294967296 | bytes 10485760 | tf_op jit(solution)/shard_map/pallas_call | solution.py:237
  72.7 1.0 %copy.8 = f32[128,2048]{1,0:T(8,128)} copy(f32[128,2048]{1,0:T(8,128)S(1)} %shard_map.64) | data formatting | bytes 2097152
Async XLA Ops:
  0.0 0.8 %copy-start = (bf16[8,2048]{1,0:T(8,128)(2,1)S(1)}, bf16[8,2048]{1,0:T(8,128)(2,1)}, u32[]{:S(2)}) copy-start(bf16[8,2048]{1,0:T(8,128)(2,1)} %amps_ref.1) | copy-start | bytes 98308
  0.8 0.7 copy-start.1
  1.4 0.7 copy-start.2
  2.1 0.7 copy-start.3
  2.8 0.7 copy-start.4

commit v2 on v0

v2 whole, which is shorter than its diff:
```python
import jax
import jax.numpy as jnp
from jax import lax
from jax.experimental import pallas as pl
from jax.experimental.pallas import tpu as pltpu
from jax.sharding import PartitionSpec as P

MESH = pl.DeviceIdType.MESH
TILE = 16
WIDTH = TILE * TILE
ROWS = 2048
TILES = ROWS // WIDTH
CD = 2048
HALF = 1024
QUARTER = 512
PAIRS = 512
SHARE = 128
NY, NZL, NX, NCORE, NOCC = 4, 2, 4, 2, 4
CHIPS = NY * NZL
CHUNK = 128
GROUP = 16
X_OFF = (0, 1, -1, 2)
BLOCKS = [(dy, dz) for dy in (0, 1, 3, 2) for dz in range(NZL)][1:]
BF16, F32 = jnp.bfloat16, jnp.float32


def kernel(
    ints_hbm, amps_hbm, tiles_hbm, pairs_hbm, e_occ_hbm, e_virt_hbm, out,
    ints, amps, tiles, pairs, e_occ, e_virt, gath, left,
    part_a, sum1_a, sum2_a, low_a, mirr_a,
    part_b, mirr_b, sum1_b, sum2_b, back_b, done_b,
    inv, pair_e, perm,
    load_sem, blk_s, blk_r, fwd_s, fwd_r, x_s, x_r, x3_s, x3_r, xf_s, xf_r, za_s, za_r, zb_s, zb_r, y_s, y_r,
):
    loop, occ = lax.axis_index("loop"), lax.axis_index("occ")
    core, x, zl, y = loop % 2, (loop // 2) % NX, (loop // 8) % NZL, loop // 16
    half = y // 2

    def at(dy=0, dz=0, dx=0, dc=0, dh=0):
        yy, zz = (y + dy + NY) % NY, (zl + dz) % NZL
        xx, cc = (x + dx + NX) % NX, (core + dc) % NCORE
        return ((yy * NZL + zz) * NX + xx) * NCORE + cc, (occ + dh + NOCC) % NOCC

    sends = []

    def send(src, dst, send_sem, recv_sem, to):
        copy = pltpu.make_async_remote_copy(
            src_ref=src, dst_ref=dst, send_sem=send_sem, recv_sem=recv_sem,
            device_id=to, device_id_type=MESH,
        )
        copy.start()
        sends.append(copy)
        return copy

    partners = [at(dc=1), at(dh=1), at(dh=-1)]
    partners += [at(dx=d) for d in X_OFF[1:]]
    partners += [at(dy=dy, dz=dz) for dy, dz in BLOCKS]
    barrier = pltpu.get_barrier_semaphore()
    for partner in partners:
        pl.semaphore_signal(barrier, inc=1, device_id=partner, device_id_type=MESH)
    loads = []
    for i, (src, dst) in enumerate((
        (amps_hbm, amps), (tiles_hbm, tiles), (pairs_hbm, pairs),
        (e_occ_hbm, e_occ), (e_virt_hbm, e_virt), (ints_hbm, ints),
    )):
        loads.append(pltpu.make_async_copy(src, dst, load_sem.at[i]))
        loads[-1].start()
    loads[0].wait()

    def block_at(dy, dz):
        return ((y + dy + NY) % NY) * NZL + (zl + dz) % NZL

    here = block_at(0, 0)
    rows8 = amps[...].astype(F32)
    gath[0, core, here] = jnp.concatenate([rows8[:, :HALF], rows8[:, HALF:]], axis=0).astype(BF16)
    pl.semaphore_wait(barrier, len(partners))

    def hand_on(i, block):
        forwards.append(send(block, block, fwd_s.at[i], fwd_r.at[i], at(dc=1)))

    def step_x(i, index):
        for j in (1, 2):
            copy = send(
                gath.at[0, core, index], gath.at[j, core, index], x_s.at[j - 1, i], x_r.at[j - 1, i], at(dx=-X_OFF[j])
            )
            chunks[j].append(copy)

    mine = gath.at[0, core, here]
    blocks, forwards, chunks = [], [], [[] for _ in range(NX)]
    for i, (dy, dz) in enumerate(BLOCKS):
        blocks.append(send(mine, mine, blk_s.at[i], blk_r.at[i], at(dy=dy, dz=dz)))
    hand_on(len(BLOCKS), mine)
    step_x(len(BLOCKS), here)
    for i, (dy, dz) in enumerate(BLOCKS):
        blocks[i].wait_recv()
        there = block_at(-dy, -dz)
        hand_on(i, gath.at[0, core, there])
        step_x(i, there)

    def spread_far():
        chunks[3].append(send(gath.at[0, core], gath.at[3, core], x3_s.at[0], x3_r.at[0], at(dx=-X_OFF[3])))

    def merge(j):
        for b in range(CHIPS):
            for h in range(2):
                lower = gath[j, 0, b].astype(F32)[8 * h:8 * h + 8]
                upper = gath[j, 1, b].astype(F32)[8 * h:8 * h + 8]
                left[h, b * GROUP:(b + 1) * GROUP, :] = jnp.concatenate([lower, upper], axis=0).astype(BF16)

    def multiply(second):
        dims = (((1,), (1,)), ((), ()))
        rows = slice(second * HALF, (second + 1) * HALF)
        product = lax.dot_general(left[0], ints[rows, :HALF], dims, preferred_element_type=F32)
        product += lax.dot_general(left[1], ints[rows, HALF:], dims, preferred_element_type=F32)
        rounded = product.astype(BF16)
        return [rounded[i * GROUP:(i + 1) * GROUP] for i in range(CHIPS)]

    def flip(blocks):
        stack = jnp.concatenate(
            [block[:, t * WIDTH:(t + 1) * WIDTH] for block in blocks for t in range(HALF // WIDTH)], axis=0
        )
        flipped = jnp.dot(stack, perm[...], preferred_element_type=F32)
        parts = [flipped[i * GROUP:(i + 1) * GROUP] for i in range(len(blocks) * (HALF // WIDTH))]
        n = HALF // WIDTH
        return [jnp.concatenate(parts[i * n:(i + 1) * n], axis=1) for i in range(len(blocks))]

    up, down, far = (occ + 1) % NOCC, (occ + 3) % NOCC, (occ + 2) % NOCC
    za = [[None] * 6 for _ in range(NX)]
    zb = [[None] * 6 for _ in range(NX)]
    ys = [[None] * 3 for _ in range(NX)]

    def out_rows(j, g):
        xx = (x + X_OFF[j] + NX) % NX
        return pl.ds(pl.multiple_of(g * 64 + xx * GROUP, GROUP), GROUP)

    def product_b(j):
        for i, block in enumerate(multiply(1)):
            part_b[j, i % 2, i // 2] = block
        ys[j][0] = send(part_b.at[j, 1 - half], mirr_b.at[j], y_s.at[j, 0], y_r.at[j, 0], at(dy=2))

    def first_b(j):
        ys[j][0].wait_recv()
        flipped = flip([mirr_b[j, k] for k in range(NOCC)])
        for k in range(NOCC):
            part_b[j, half, k] = (part_b[j, half, k].astype(F32) + flipped[k]).astype(BF16)
        plan = [
            (part_b.at[j, half, far, :, :QUARTER], sum1_b.at[j, 0], 1),
            (part_b.at[j, half, far, :, QUARTER:], sum1_b.at[j, 1], -1),
            (part_b.at[j, half, up, :, QUARTER:], sum2_b.at[j, 0, 1], 1),
            (part_b.at[j, half, down, :, :QUARTER], sum2_b.at[j, 1, 0], -1),
        ]
        for i, (src, dst, to) in enumerate(plan):
            zb[j][i] = send(src, dst, zb_s.at[j, i], zb_r.at[j, i], at(dh=to))

    def second_b(j):
        for i, who, columns, to in ((0, up, slice(0, QUARTER), 1), (1, down, slice(QUARTER, HALF), -1)):
            zb[j][i].wait_recv()
            total = part_b[j, half, who, :, columns].astype(F32) + sum1_b[j, i].astype(F32)
            part_b[j, half, who, :, columns] = total.astype(BF16)
            zb[j][4 + i] = send(
                part_b.at[j, half, who, :, columns], sum2_b.at[j, i, i], zb_s.at[j, 4 + i], zb_r.at[j, 4 + i], at(dh=to)
            )

    def total_b(j):
        for i in range(2, 6):
            zb[j][i].wait_recv()
        both = [jnp.concatenate([sum2_b[j, i, 0], sum2_b[j, i, 1]], axis=1).astype(F32) for i in range(2)]
        total = part_b[j, half, occ].astype(F32) + both[0] + both[1]
        back_b[j] = total.astype(BF16)
        ys[j][2] = send(back_b.at[j], done_b.at[j], y_s.at[j, 2], y_r.at[j, 2], at(dy=2))
        rows = out_rows(j, half)
        out[rows, HALF:] = total * inv[rows, HALF:]

    def finish_b(j):
        ys[j][2].wait_recv()
        rows = out_rows(j, 1 - half)
        out[rows, HALF:] = flip([done_b[j]])[0] * inv[rows, HALF:]

    def product_a(j):
        for i, block in enumerate(multiply(0)):
            part_a[j, i // 2, i % 2] = block
        plan = [
            (part_a.at[j, far, 0], sum1_a.at[j, 0], 1),
            (part_a.at[j, far, 1], sum1_a.at[j, 1], -1),
            (part_a.at[j, up, 1], sum2_a.at[j, 0, 1], 1),
            (part_a.at[j, down, 0], sum2_a.at[j, 1, 0], -1),
        ]
        for i, (src, dst, to) in enumerate(plan):
            za[j][i] = send(src, dst, za_s.at[j, i], za_r.at[j, i], at(dh=to))

    def second_a(j):
        for i, who, to in ((0, up, 1), (1, down, -1)):
            za[j][i].wait_recv()
            part_a[j, who, i] = (part_a[j, who, i].astype(F32) + sum1_a[j, i].astype(F32)).astype(BF16)
            za[j][4 + i] = send(part_a.at[j, who, i], sum2_a.at[j, i, i], za_s.at[j, 4 + i], za_r.at[j, 4 + i], at(dh=to))

    def total_a(j):
        for i in range(2, 6):
            za[j][i].wait_recv()
        for g in range(2):
            total = part_a[j, occ, g].astype(F32) + sum2_a[j, 0, g].astype(F32) + sum2_a[j, 1, g].astype(F32)
            out[out_rows(j, g), :HALF] = total
            low_a[j, g] = total.astype(BF16)
        ys[j][1] = send(low_a.at[j], mirr_a.at[j], y_s.at[j, 1], y_r.at[j, 1], at(dy=2))

    def finish_a(j):
        ys[j][1].wait_recv()
        flipped = flip([mirr_a[j, g] for g in range(2)])
        for g in range(2):
            rows = out_rows(j, g)
            out[rows, :HALF] = (out[rows, :HALF] + flipped[g]) * inv[rows, :HALF]

    siblings = [None] * NX

    def pass_on(j):
        for copy in chunks[j]:
            copy.wait_recv()
        there = gath.at[j, core]
        siblings[j] = send(there, there, xf_s.at[j - 1], xf_r.at[j - 1], at(dc=1))

    def arrive(j):
        siblings[j].wait_recv()
        merge(j)

    def energies():
        for load in loads[1:5]:
            load.wait()
        sub = lax.broadcasted_iota(jnp.int32, (8, 128), 0)

        def pair_body(g, carry):
            rows = jnp.zeros((8, 128), F32)
            for i in range(8):
                pair = occ * SHARE + g * 8 + i
                energy = e_occ[pairs[0, pair]] + e_occ[pairs[1, pair]]
                rows = jnp.where(sub == i, energy, rows)
            pair_e[pl.ds(pl.multiple_of(g * 8, 8), 8), :] = rows
            return carry

        lax.fori_loop(0, SHARE // 8, pair_body, 0)
        lane = lax.broadcasted_iota(jnp.int32, (8, WIDTH), 1)
        lane_x, lane_y = lane // TILE, lane % TILE

        def tile_body(t, carry):
            first, second = tiles[0, t], tiles[1, t]
            a, b = jnp.maximum(first, 0) * TILE, jnp.maximum(second, 0) * TILE
            e_a = jnp.zeros((8, WIDTH), F32)
            e_b = jnp.zeros((8, WIDTH), F32)
            for i in range(TILE):
                e_a = jnp.where(lane_x == i, e_virt[a + i], e_a)
                e_b = jnp.where(lane_y == i, e_virt[b + i], e_b)
            energy = e_a + e_b
            keep = jnp.full((8, WIDTH), first, jnp.int32) >= 0
            columns = pl.ds(pl.multiple_of(t * WIDTH, WIDTH), WIDTH)
            for g in range(SHARE // 8):
                pair = pair_e[g * 8:(g + 1) * 8, :]
                denom = jnp.concatenate([pair, pair], axis=1) - energy
                inv[g * 8:(g + 1) * 8, columns] = jnp.where(keep, 1.0 / denom, 0.0)
            return carry

        lax.fori_loop(0, TILES, tile_body, 0)

    row_at = lax.broadcasted_iota(jnp.int32, (WIDTH, WIDTH), 0)
    col_at = lax.broadcasted_iota(jnp.int32, (WIDTH, WIDTH), 1)
    perm[...] = jnp.where(col_at == (row_at % TILE) * TILE + row_at // TILE, 1.0, 0.0).astype(BF16)
    for copy in forwards:
        copy.wait_recv()
    merge(0)
    loads[5].wait()
    product_b(0)
    product_a(0)
    spread_far()
    pass_on(1)
    energies()
    arrive(1)
    product_b(1)
    pass_on(2)
    product_a(1)
    first_b(0)
    second_a(0)
    arrive(2)
    product_b(2)
    pass_on(3)
    product_a(2)
    second_b(0)
    total_a(0)
    first_b(1)
    second_a(1)
    arrive(3)
    product_b(3)
    product_a(3)
    total_b(0)
    finish_a(0)
    second_b(1)
    total_a(1)
    first_b(2)
    second_a(2)
    finish_b(0)
    total_b(1)
    finish_a(1)
    second_b(2)
    total_a(2)
    first_b(3)
    second_a(3)
    finish_b(1)
    total_b(2)
    finish_a(2)
    second_b(3)
    total_a(3)
    finish_b(2)
    total_b(3)
    finish_a(3)
    finish_b(3)
    for copy in sends:
        copy.wait_send()


def per_device(integrals, amplitudes, tile_list, occ_pairs, e_occ, e_virt):
    dma = pltpu.SemaphoreType.DMA
    vmem, smem = pltpu.VMEM, pltpu.SMEM
    n_blocks = len(BLOCKS)
    operands = integrals, amplitudes, tile_list.T, occ_pairs.T, e_occ, e_virt
    operands = [pltpu.with_memory_space_constraint(operand, pltpu.HBM) for operand in operands]
    return pl.pallas_call(
        kernel,
        out_shape=jax.ShapeDtypeStruct((SHARE, ROWS), F32),
        in_specs=[pl.BlockSpec(memory_space=pltpu.HBM)] * 6,
        out_specs=pl.BlockSpec(memory_space=vmem),
        scratch_shapes=[
            vmem((ROWS, CD), BF16),
            vmem((8, CD), BF16),
            smem((2, TILES), jnp.int32),
            smem((2, PAIRS), jnp.int32),
            smem(e_occ.shape, F32),
            smem(e_virt.shape, F32),
            vmem((NX, NCORE, CHIPS, GROUP, HALF), BF16),
            vmem((2, CHUNK, HALF), BF16),
            vmem((NX, NOCC, 2, GROUP, HALF), BF16),
            vmem((NX, 2, GROUP, HALF), BF16),
            vmem((NX, 2, 2, GROUP, HALF), BF16),
            vmem((NX, 2, GROUP, HALF), BF16),
            vmem((NX, 2, GROUP, HALF), BF16),
            vmem((NX, 2, NOCC, GROUP, HALF), BF16),
            vmem((NX, NOCC, GROUP, HALF), BF16),
            vmem((NX, 2, GROUP, QUARTER), BF16),
            vmem((NX, 2, 2, GROUP, QUARTER), BF16),
            vmem((NX, GROUP, HALF), BF16),
            vmem((NX, GROUP, HALF), BF16),
            vmem((SHARE, ROWS), F32),
            vmem((SHARE, 128), F32),
            vmem((WIDTH, WIDTH), BF16),
            dma((6,)),
            dma((n_blocks,)), dma((n_blocks,)),
            dma((n_blocks + 1,)), dma((n_blocks + 1,)),
            dma((2, n_blocks + 1)), dma((2, n_blocks + 1)),
            dma((1,)), dma((1,)),
            dma((NX - 1,)), dma((NX - 1,)),
            dma((NX, 6)), dma((NX, 6)),
            dma((NX, 6)), dma((NX, 6)),
            dma((NX, 3)), dma((NX, 3)),
        ],
        compiler_params=pltpu.CompilerParams(
            collective_id=0, has_side_effects=True, vmem_limit_bytes=48 << 20
        ),
        cost_estimate=pl.CostEstimate(flops=2 * PAIRS * ROWS * CD, bytes_accessed=10 << 20, transcendentals=0),
    )(*operands)


def solution(mesh):
    placed = (P("loop", "occ"), P("loop", "occ"), P("loop", None), P(), P(), P())
    return jax.shard_map(
        per_device, mesh=mesh, in_specs=placed, out_specs=P("occ", "loop"), check_vma=False
    )
```

time: 256 us -> 59.8 us (0.23)
  waiting for transfers between devices: 207 us -> 0 us
  Pallas kernels: 0 us -> 58.7 us
  local copies, waits for them, and re-layouts: 16.7 us -> 0.97 us
  between operations: 13.5 us -> 0.01 us
  matrix products: 8.54 us -> 0 us
  other arithmetic: 7.07 us -> 0 us
    all_gather x1 -> x0, waiting for transfers between devices: 110 us -> none  [per_device(): lax.all_gather(amplitudes, 'loop', axis=0, tiled=True)]
    pallas_call x0 -> x1, Pallas kernels: none -> 58.7 us  [per_device(): pl.pallas_call(kernel, out_shape=jax.ShapeDtypeStruct((SHARE, ROWS), F32)...]
    reduce_scatter x1 -> x0, waiting for transfers between devices: 49.5 us -> none  [per_device(): lax.psum_scatter(combined.astype(jnp.bfloat16), 'occ', scatter_dimension=...]
    ppermute x1 -> x0, waiting for transfers between devices: 47.2 us -> none  [shifted(): lax.ppermute(array, axis, [(i, (i + by) % devices) for i in range(devices)])]
    convert_element_type x3 -> x0, local copies, waits for them, and re-layouts: 15.1 us -> none  [per_device(): flip_tiles(mirrored, tiles).astype(jnp.float32)]
    dot_general x1 -> x0, matrix products: 8.54 us -> none  [per_device(): lax.dot_general(lax.all_gather(amplitudes, 'loop', axis=0, tiled=True), i...]
    convert_element_type x1 -> x0, other arithmetic: 4.25 us -> none  [per_device(): combined.astype(jnp.bfloat16)]
  transfers between devices with their start and end apart: 3 -> 0, of which waited for: 3 -> 0; matrix products, arithmetic and copies ran while one was open for 0% -> 0% of each run, Pallas kernels for 0% -> 0%
where the time goes in v2:
time: 59.8 us; the launch traced here: 59.7 us
  Pallas kernels  58.7 us (98%)
  local copies, waits for them, and re-layouts  0.97 us (2%)
    pallas_call x1, Pallas kernels, per_device(): pl.pallas_call(kernel, out_shape=jax.ShapeDtypeStruct((SHARE, ROWS), F32)...  58.7 us

profile of v2, /device:TPU:4, one launch (start us, length us, event | category | flops | bytes accessed | tf_op | source)
XLA Modules:
  0.0 59.7 jit_solution(5415697744983570111)
XLA Ops:
  0.0 58.7 %shard_map.64 = f32[128,2048]{1,0:T(8,128)S(1)} custom-call(bf16[2048,2048]{1,0:T(8,128)(2,1)} %ints_hbm.1, bf16[8,2048]{1,0:T(8,128)(2,1)} %amps_hbm.1, s32[2,8]{1,0:T(2,128)} %bitcast.3, s32[2,512]{1,0:T(2,128)} %bitcast.2, f32[200]{0:T(256)} %e_occ_hbm.1, f32[800]{0:T(1024)} %e_virt_hbm.1), custom_call_target="tpu_custom_call" | custom-call | flops 4294967296 | bytes 10485760 | tf_op jit(solution)/shard_map/pallas_call | solution.py:323
  58.7 1.0 %copy.8 = f32[128,2048]{1,0:T(8,128)} copy(f32[128,2048]{1,0:T(8,128)S(1)} %shard_map.64) | data formatting | bytes 2097152

commit v3 on v2

--- a/solution.py
+++ b/solution.py
@@ -12,7 +12,9 @@
 TILES = ROWS // WIDTH
 CD = 2048
 HALF = 1024
-QUARTER = 512
+COLS_A = 3 * WIDTH
+COLS_B = ROWS - COLS_A
+MID = COLS_B // 2
 PAIRS = 512
 SHARE = 128
 NY, NZL, NX, NCORE, NOCC = 4, 2, 4, 2, 4
@@ -53,7 +55,7 @@
         return copy
 
     partners = [at(dc=1), at(dh=1), at(dh=-1)]
-    partners += [at(dx=d) for d in X_OFF[1:]]
+    partners += [at(dx=1), at(dx=-1)]
     partners += [at(dy=dy, dz=dz) for dy, dz in BLOCKS]
     barrier = pltpu.get_barrier_semaphore()
     for partner in partners:
@@ -97,31 +99,33 @@
         hand_on(i, gath.at[0, core, there])
         step_x(i, there)
 
-    def spread_far():
-        chunks[3].append(send(gath.at[0, core], gath.at[3, core], x3_s.at[0], x3_r.at[0], at(dx=-X_OFF[3])))
-
-    def merge(j):
+    def relay():
+        part = slice(0, CHIPS // 2)
+        chunks[3].append(send(gath.at[1, core, part], gath.at[3, core, part], x3_s.at[0], x3_r.at[0], at(dx=-1)))
+        part = slice(CHIPS // 2, CHIPS)
+        chunks[3].append(send(gath.at[2, core, part], gath.at[3, core, part], x3_s.at[1], x3_r.at[1], at(dx=1)))
+
+    def merge(j, slot):
         for b in range(CHIPS):
             for h in range(2):
                 lower = gath[j, 0, b].astype(F32)[8 * h:8 * h + 8]
                 upper = gath[j, 1, b].astype(F32)[8 * h:8 * h + 8]
-                left[h, b * GROUP:(b + 1) * GROUP, :] = jnp.concatenate([lower, upper], axis=0).astype(BF16)
-
-    def multiply(second):
+                rows = slice(slot * CHUNK + b * GROUP, slot * CHUNK + (b + 1) * GROUP)
+                left[h, rows, :] = jnp.concatenate([lower, upper], axis=0).astype(BF16)
+
+    def multiply(rows, chunks):
         dims = (((1,), (1,)), ((), ()))
-        rows = slice(second * HALF, (second + 1) * HALF)
-        product = lax.dot_general(left[0], ints[rows, :HALF], dims, preferred_element_type=F32)
-        product += lax.dot_general(left[1], ints[rows, HALF:], dims, preferred_element_type=F32)
+        here = slice(0, chunks * CHUNK)
+        product = lax.dot_general(left[0, here], ints[rows, :HALF], dims, preferred_element_type=F32)
+        product += lax.dot_general(left[1, here], ints[rows, HALF:], dims, preferred_element_type=F32)
         rounded = product.astype(BF16)
-        return [rounded[i * GROUP:(i + 1) * GROUP] for i in range(CHIPS)]
+        return [rounded[i * GROUP:(i + 1) * GROUP] for i in range(chunks * CHIPS)]
 
     def flip(blocks):
-        stack = jnp.concatenate(
-            [block[:, t * WIDTH:(t + 1) * WIDTH] for block in blocks for t in range(HALF // WIDTH)], axis=0
-        )
+        n = blocks[0].shape[1] // WIDTH
+        stack = jnp.concatenate([block[:, t * WIDTH:(t + 1) * WIDTH] for block in blocks for t in range(n)], axis=0)
         flipped = jnp.dot(stack, perm[...], preferred_element_type=F32)
-        parts = [flipped[i * GROUP:(i + 1) * GROUP] for i in range(len(blocks) * (HALF // WIDTH))]
-        n = HALF // WIDTH
+        parts = [flipped[i * GROUP:(i + 1) * GROUP] for i in range(len(blocks) * n)]
         return [jnp.concatenate(parts[i * n:(i + 1) * n], axis=1) for i in range(len(blocks))]
 
     up, down, far = (occ + 1) % NOCC, (occ + 3) % NOCC, (occ + 2) % NOCC
@@ -133,10 +137,12 @@
         xx = (x + X_OFF[j] + NX) % NX
         return pl.ds(pl.multiple_of(g * 64 + xx * GROUP, GROUP), GROUP)
 
-    def product_b(j):
-        for i, block in enumerate(multiply(1)):
-            part_b[j, i % 2, i // 2] = block
-        ys[j][0] = send(part_b.at[j, 1 - half], mirr_b.at[j], y_s.at[j, 0], y_r.at[j, 0], at(dy=2))
+    def product_b(*js):
+        found = multiply(slice(COLS_A, ROWS), len(js))
+        for n, j in enumerate(js):
+            for i in range(CHIPS):
+                part_b[j, i % 2, i // 2] = found[n * CHIPS + i]
+            ys[j][0] = send(part_b.at[j, 1 - half], mirr_b.at[j], y_s.at[j, 0], y_r.at[j, 0], at(dy=2))
 
     def first_b(j):
         ys[j][0].wait_recv()
@@ -144,16 +150,16 @@
         for k in range(NOCC):
             part_b[j, half, k] = (part_b[j, half, k].astype(F32) + flipped[k]).astype(BF16)
         plan = [
-            (part_b.at[j, half, far, :, :QUARTER], sum1_b.at[j, 0], 1),
-            (part_b.at[j, half, far, :, QUARTER:], sum1_b.at[j, 1], -1),
-            (part_b.at[j, half, up, :, QUARTER:], sum2_b.at[j, 0, 1], 1),
-            (part_b.at[j, half, down, :, :QUARTER], sum2_b.at[j, 1, 0], -1),
+            (part_b.at[j, half, far, :, :MID], sum1_b.at[j, 0], 1),
+            (part_b.at[j, half, far, :, MID:], sum1_b.at[j, 1], -1),
+            (part_b.at[j, half, up, :, MID:], sum2_b.at[j, 0, 1], 1),
+            (part_b.at[j, half, down, :, :MID], sum2_b.at[j, 1, 0], -1),
         ]
         for i, (src, dst, to) in enumerate(plan):
             zb[j][i] = send(src, dst, zb_s.at[j, i], zb_r.at[j, i], at(dh=to))
 
     def second_b(j):
-        for i, who, columns, to in ((0, up, slice(0, QUARTER), 1), (1, down, slice(QUARTER, HALF), -1)):
+        for i, who, columns, to in ((0, up, slice(0, MID), 1), (1, down, slice(MID, COLS_B), -1)):
             zb[j][i].wait_recv()
             total = part_b[j, half, who, :, columns].astype(F32) + sum1_b[j, i].astype(F32)
             part_b[j, half, who, :, columns] = total.astype(BF16)
@@ -169,24 +175,26 @@
         back_b[j] = total.astype(BF16)
         ys[j][2] = send(back_b.at[j], done_b.at[j], y_s.at[j, 2], y_r.at[j, 2], at(dy=2))
         rows = out_rows(j, half)
-        out[rows, HALF:] = total * inv[rows, HALF:]
+        out[rows, COLS_A:] = total * inv[rows, COLS_A:]
 
     def finish_b(j):
         ys[j][2].wait_recv()
         rows = out_rows(j, 1 - half)
-        out[rows, HALF:] = flip([done_b[j]])[0] * inv[rows, HALF:]
-
-    def product_a(j):
-        for i, block in enumerate(multiply(0)):
-            part_a[j, i // 2, i % 2] = block
-        plan = [
-            (part_a.at[j, far, 0], sum1_a.at[j, 0], 1),
-            (part_a.at[j, far, 1], sum1_a.at[j, 1], -1),
-            (part_a.at[j, up, 1], sum2_a.at[j, 0, 1], 1),
-            (part_a.at[j, down, 0], sum2_a.at[j, 1, 0], -1),
-        ]
-        for i, (src, dst, to) in enumerate(plan):
-            za[j][i] = send(src, dst, za_s.at[j, i], za_r.at[j, i], at(dh=to))
+        out[rows, COLS_A:] = flip([done_b[j]])[0] * inv[rows, COLS_A:]
+
+    def product_a(*js):
+        found = multiply(slice(0, COLS_A), len(js))
+        for n, j in enumerate(js):
+            for i in range(CHIPS):
+                part_a[j, i // 2, i % 2] = found[n * CHIPS + i]
+            plan = [
+                (part_a.at[j, far, 0], sum1_a.at[j, 0], 1),
+                (part_a.at[j, far, 1], sum1_a.at[j, 1], -1),
+                (part_a.at[j, up, 1], sum2_a.at[j, 0, 1], 1),
+                (part_a.at[j, down, 0], sum2_a.at[j, 1, 0], -1),
+            ]
+            for i, (src, dst, to) in enumerate(plan):
+                za[j][i] = send(src, dst, za_s.at[j, i], za_r.at[j, i], at(dh=to))
 
     def second_a(j):
         for i, who, to in ((0, up, 1), (1, down, -1)):
@@ -199,7 +207,7 @@
             za[j][i].wait_recv()
         for g in range(2):
             total = part_a[j, occ, g].astype(F32) + sum2_a[j, 0, g].astype(F32) + sum2_a[j, 1, g].astype(F32)
-            out[out_rows(j, g), :HALF] = total
+            out[out_rows(j, g), :COLS_A] = total
             low_a[j, g] = total.astype(BF16)
         ys[j][1] = send(low_a.at[j], mirr_a.at[j], y_s.at[j, 1], y_r.at[j, 1], at(dy=2))
 
@@ -208,7 +216,7 @@
         flipped = flip([mirr_a[j, g] for g in range(2)])
         for g in range(2):
             rows = out_rows(j, g)
-            out[rows, :HALF] = (out[rows, :HALF] + flipped[g]) * inv[rows, :HALF]
+            out[rows, :COLS_A] = (out[rows, :COLS_A] + flipped[g]) * inv[rows, :COLS_A]
 
     siblings = [None] * NX
 
@@ -218,9 +226,9 @@
         there = gath.at[j, core]
         siblings[j] = send(there, there, xf_s.at[j - 1], xf_r.at[j - 1], at(dc=1))
 
-    def arrive(j):
+    def arrive(j, slot):
         siblings[j].wait_recv()
-        merge(j)
+        merge(j, slot)
 
     def energies():
         for load in loads[1:5]:
@@ -264,51 +272,51 @@
     perm[...] = jnp.where(col_at == (row_at % TILE) * TILE + row_at // TILE, 1.0, 0.0).astype(BF16)
     for copy in forwards:
         copy.wait_recv()
-    merge(0)
+    merge(0, 0)
     loads[5].wait()
+    product_a(0)
+    pass_on(1)
     product_b(0)
-    product_a(0)
-    spread_far()
-    pass_on(1)
-    energies()
-    arrive(1)
+    pass_on(2)
+    relay()
+    arrive(1, 0)
+    product_a(1)
+    second_a(0)
     product_b(1)
-    pass_on(2)
-    product_a(1)
     first_b(0)
-    second_a(0)
-    arrive(2)
+    arrive(2, 0)
+    product_a(2)
+    second_a(1)
     product_b(2)
     pass_on(3)
-    product_a(2)
+    first_b(1)
+    arrive(3, 0)
+    product_a(3)
+    second_a(2)
+    product_b(3)
+    energies()
     second_b(0)
     total_a(0)
-    first_b(1)
-    second_a(1)
-    arrive(3)
-    product_b(3)
-    product_a(3)
+    first_b(2)
+    second_a(3)
+    total_a(1)
+    second_b(1)
+    first_b(3)
+    total_a(2)
     total_b(0)
+    second_b(2)
     finish_a(0)
-    second_b(1)
-    total_a(1)
-    first_b(2)
-    second_a(2)
+    total_a(3)
+    total_b(1)
+    second_b(3)
+    finish_a(1)
     finish_b(0)
-    total_b(1)
-    finish_a(1)
-    second_b(2)
-    total_a(2)
-    first_b(3)
-    second_a(3)
-    finish_b(1)
     total_b(2)
     finish_a(2)
-    second_b(3)
-    total_a(3)
+    finish_b(1)
+    finish_a(3)
+    total_b(3)
     finish_b(2)
-    total_b(3)
-    finish_a(3)
     finish_b(3)
     for copy in sends:
         copy.wait_send()
@@ -333,18 +341,18 @@
             smem(e_occ.shape, F32),
             smem(e_virt.shape, F32),
             vmem((NX, NCORE, CHIPS, GROUP, HALF), BF16),
-            vmem((2, CHUNK, HALF), BF16),
-            vmem((NX, NOCC, 2, GROUP, HALF), BF16),
-            vmem((NX, 2, GROUP, HALF), BF16),
-            vmem((NX, 2, 2, GROUP, HALF), BF16),
-            vmem((NX, 2, GROUP, HALF), BF16),
-            vmem((NX, 2, GROUP, HALF), BF16),
-            vmem((NX, 2, NOCC, GROUP, HALF), BF16),
-            vmem((NX, NOCC, GROUP, HALF), BF16),
-            vmem((NX, 2, GROUP, QUARTER), BF16),
-            vmem((NX, 2, 2, GROUP, QUARTER), BF16),
-            vmem((NX, GROUP, HALF), BF16),
-            vmem((NX, GROUP, HALF), BF16),
+            vmem((2, 2 * CHUNK, HALF), BF16),
+            vmem((NX, NOCC, 2, GROUP, COLS_A), BF16),
+            vmem((NX, 2, GROUP, COLS_A), BF16),
+            vmem((NX, 2, 2, GROUP, COLS_A), BF16),
+            vmem((NX, 2, GROUP, COLS_A), BF16),
+            vmem((NX, 2, GROUP, COLS_A), BF16),
+            vmem((NX, 2, NOCC, GROUP, COLS_B), BF16),
+            vmem((NX, NOCC, GROUP, COLS_B), BF16),
+            vmem((NX, 2, GROUP, MID), BF16),
+            vmem((NX, 2, 2, GROUP, MID), BF16),
+            vmem((NX, GROUP, COLS_B), BF16),
+            vmem((NX, GROUP, COLS_B), BF16),
             vmem((SHARE, ROWS), F32),
             vmem((SHARE, 128), F32),
             vmem((WIDTH, WIDTH), BF16),
@@ -352,7 +360,7 @@
             dma((n_blocks,)), dma((n_blocks,)),
             dma((n_blocks + 1,)), dma((n_blocks + 1,)),
             dma((2, n_blocks + 1)), dma((2, n_blocks + 1)),
-            dma((1,)), dma((1,)),
+            dma((2,)), dma((2,)),
             dma((NX - 1,)), dma((NX - 1,)),
             dma((NX, 6)), dma((NX, 6)),
             dma((NX, 6)), dma((NX, 6)),

time: 59.8 us -> 54 us (0.903); the launches traced: 59.7 us -> 53.1 us
  Pallas kernels: 58.7 us -> 52.2 us
    pallas_call x1, Pallas kernels: 58.7 us -> 52.2 us  [per_device(): pl.pallas_call(kernel, out_shape=jax.ShapeDtypeStruct((SHARE, ROWS), F32)...]
where the time goes in v3:
time: 54 us; the launch traced here: 53.1 us
  Pallas kernels  52.2 us (97%)
  local copies, waits for them, and re-layouts  0.97 us (2%)
    pallas_call x1, Pallas kernels, per_device(): pl.pallas_call(kernel, out_shape=jax.ShapeDtypeStruct((SHARE, ROWS), F32)...  52.2 us

profile of v3, /device:TPU:4, one launch (start us, length us, event | category | flops | bytes accessed | tf_op | source)
XLA Modules:
  0.0 53.1 jit_solution(8985655918013446357)
XLA Ops:
  0.0 52.2 %shard_map.64 = f32[128,2048]{1,0:T(8,128)S(1)} custom-call(bf16[2048,2048]{1,0:T(8,128)(2,1)} %ints_hbm.1, bf16[8,2048]{1,0:T(8,128)(2,1)} %amps_hbm.1, s32[2,8]{1,0:T(2,128)} %bitcast.3, s32[2,512]{1,0:T(2,128)} %bitcast.2, f32[200]{0:T(256)} %e_occ_hbm.1, f32[800]{0:T(1024)} %e_virt_hbm.1), custom_call_target="tpu_custom_call" | custom-call | flops 4294967296 | bytes 10485760 | tf_op jit(solution)/shard_map/pallas_call | solution.py:331
  52.2 1.0 %copy.8 = f32[128,2048]{1,0:T(8,128)} copy(f32[128,2048]{1,0:T(8,128)S(1)} %shard_map.64) | data formatting | bytes 2097152

commit v4 on v3

--- a/solution.py
+++ b/solution.py
@@ -54,12 +54,6 @@
         sends.append(copy)
         return copy
 
-    partners = [at(dc=1), at(dh=1), at(dh=-1)]
-    partners += [at(dx=1), at(dx=-1)]
-    partners += [at(dy=dy, dz=dz) for dy, dz in BLOCKS]
-    barrier = pltpu.get_barrier_semaphore()
-    for partner in partners:
-        pl.semaphore_signal(barrier, inc=1, device_id=partner, device_id_type=MESH)
     loads = []
     for i, (src, dst) in enumerate((
         (amps_hbm, amps), (tiles_hbm, tiles), (pairs_hbm, pairs),
@@ -67,6 +61,12 @@
     )):
         loads.append(pltpu.make_async_copy(src, dst, load_sem.at[i]))
         loads[-1].start()
+    partners = [at(dc=1), at(dh=1), at(dh=-1)]
+    partners += [at(dx=1), at(dx=-1)]
+    partners += [at(dy=dy, dz=dz) for dy, dz in BLOCKS]
+    barrier = pltpu.get_barrier_semaphore()
+    for partner in partners:
+        pl.semaphore_signal(barrier, inc=1, device_id=partner, device_id_type=MESH)
     loads[0].wait()
 
     def block_at(dy, dz):
@@ -96,8 +96,8 @@
     for i, (dy, dz) in enumerate(BLOCKS):
         blocks[i].wait_recv()
         there = block_at(-dy, -dz)
+        step_x(i, there)
         hand_on(i, gath.at[0, core, there])
-        step_x(i, there)
 
     def relay():
         part = slice(0, CHIPS // 2)

time: 54 us -> 53.9 us (level)
  no operation moved by 1% of the time
where the time goes in v4:
time: 53.9 us; the launch traced here: 53 us
  Pallas kernels  52 us (96%)
  local copies, waits for them, and re-layouts  0.97 us (2%)
    pallas_call x1, Pallas kernels, per_device(): pl.pallas_call(kernel, out_shape=jax.ShapeDtypeStruct((SHARE, ROWS), F32)...  52 us

profile of v4, /device:TPU:4, one launch (start us, length us, event | category | flops | bytes accessed | tf_op | source)
XLA Modules:
  0.0 53.0 jit_solution(13844502708414155623)
XLA Ops:
  0.0 52.0 %shard_map.64 = f32[128,2048]{1,0:T(8,128)S(1)} custom-call(bf16[2048,2048]{1,0:T(8,128)(2,1)} %ints_hbm.1, bf16[8,2048]{1,0:T(8,128)(2,1)} %amps_hbm.1, s32[2,8]{1,0:T(2,128)} %bitcast.3, s32[2,512]{1,0:T(2,128)} %bitcast.2, f32[200]{0:T(256)} %e_occ_hbm.1, f32[800]{0:T(1024)} %e_virt_hbm.1), custom_call_target="tpu_custom_call" | custom-call | flops 4294967296 | bytes 10485760 | tf_op jit(solution)/shard_map/pallas_call | solution.py:331
  52.0 1.0 %copy.8 = f32[128,2048]{1,0:T(8,128)} copy(f32[128,2048]{1,0:T(8,128)S(1)} %shard_map.64) | data formatting | bytes 2097152
